TPU v7x, 512 devices: a whole 4x4x16 slice. The times are simulated.
512 devices in a mesh: pair: 8 (over z_hi, y), blk: 64 (over z_lo, x, core).
Axes of the slice: x: 4, y: 4, z: 16 (z_hi: 2, z_lo: 8; z = z_hi * 8 + z_lo), core: 2. Of those that a mesh axis runs over, the one named last changes fastest.
Arguments:
- amps: bfloat16 [8192, 80200], P(('blk', 'pair')), may hold values from -6 to 6
- ints: bfloat16 [1024, 80200], P('blk', 'pair'), may hold values from -0.015625 to 0.015625
- block_of: int32 [64], replicated, may hold values from 0 to 63, each once
- pair_rows: int32 [8192, 2], P(('blk', 'pair')), may hold values from 0 to 119
- occ_energy: float32 [120], replicated, may hold values from -2 to -0.5
- vir_pair_energy: float32 [1024], replicated, may hold values from 1 to 6
Outputs:
- new_amps: float32 [8192, 1024], P(('blk', 'pair'))
Inputs may be any that keep to these rules, and one draw needn't show every extreme that they name: `block_of`: each of 0 to 63 once.
All inputs are finite; a program needn't handle non-finite values.
Results may differ from a plain program's by a relative error of at most 0.0003.
Values may be sent and summed in bfloat16 or wider, within the bound.
A program may use at most 128 MiB of HBM per device.

v0:
```python
import jax
import jax.numpy as jnp
from jax import lax
from jax.sharding import PartitionSpec as P

NV = 400


def contract(weighted, slab_part):
    return lax.dot_general(
        weighted, slab_part, (((1,), (1,)), ((), ())), preferred_element_type=jnp.float32
    )


def per_device(amps, ints, block_of, pair_rows, occ_energy, vir_pair_energy):
    relaid = lax.all_to_all(amps, "pair", split_axis=1, concat_axis=0, tiled=True)
    shard_width = relaid.shape[1]
    column = lax.axis_index("pair") * shard_width + lax.broadcasted_iota(
        jnp.int32, (1, shard_width), 1
    )
    weighted = relaid * jnp.where(column < NV, 1.0, 2.0).astype(jnp.bfloat16)
    gathered = lax.all_gather(ints, "blk", axis=0, tiled=True)
    stored = contract(weighted, gathered)
    summed = lax.psum_scatter(stored, "pair", scatter_dimension=0, tiled=True)
    blocks = block_of.shape[0]
    height = summed.shape[0]
    grouped = summed.reshape(height, blocks, summed.shape[1] // blocks)
    ladder = jnp.zeros_like(grouped).at[:, block_of].set(grouped).reshape(height, summed.shape[1])
    levels = lax.broadcasted_iota(jnp.int32, (1, 1, occ_energy.shape[0]), 2)
    one_hot = (pair_rows[:, :, None] == levels).astype(jnp.float32)
    occupied = jnp.sum(one_hot * occ_energy[None, None, :], axis=(1, 2))
    denominator = vir_pair_energy[None, :] - occupied[:, None]
    return ladder / denominator


def solution(mesh):
    placed = (P(("blk", "pair"), None), P("blk", "pair"), P(), P(("blk", "pair"), None), P(), P())
    return jax.shard_map(
        per_device, mesh=mesh, in_specs=placed, out_specs=P(("blk", "pair"), None), check_vma=False
    )
```

profile of v0, /device:TPU:2, one launch (start us, length us, event | category | flops | bytes accessed | tf_op | source)
XLA Modules:
  0.0 403.6 jit_solution(10764181286795484275)
XLA Ops:
  6.5 0.0 all-gather.2.cloned.1.call-start
  6.5 0.7 all-gather.2.cloned.1.call-update
  7.3 4.8 %all_to_all.14 = bf16[16,8,10025]{2,1,0:T(8,128)(2,1)S(1)} reshape(bf16[16,80200]{1,0:T(8,128)(2,1)} %param.6) | data formatting | bytes 5132800 | tf_op jit(solution)/shard_map/all_to_all | solution.py:16
  12.1 1.8 copy.13
  13.9 17.7 %all-to-all-start = ((bf16[16,8,10025]{2,0,1:T(8,128)(2,1)}), bf16[16,8,10025]{2,0,1:T(8,128)(2,1)}, u32[]{:S(2)}, u32[]{:S(2)}) async-start(bf16[16,8,10025]{2,0,1:T(8,128)(2,1)} %copy.13), calls=%async_computation | async-start | bytes 5177344 | tf_op jit(solution)/shard_map/all_to_all | solution.py:16
  31.6 0.0 reduce-scatter.2.cloned.1.call-start
  31.7 66.3 %all-to-all-done = bf16[16,8,10025]{2,0,1:T(8,128)(2,1)} async-done(((bf16[16,8,10025]{2,0,1:T(8,128)(2,1)}), bf16[16,8,10025]{2,0,1:T(8,128)(2,1)}, u32[]{:S(2)}, u32[]{:S(2)}) %all-to-all-start) | async-done | bytes 2566432 | tf_op jit(solution)/shard_map/all_to_all | solution.py:16
  97.9 2.1 bitcast_multiply_fusion
  100.0 0.0 copy-start.1
  100.0 0.0 copy-start.2
  100.1 0.0 copy-start.3
  100.1 166.9 %all-gather.2.cloned.1.call-done = bf16[1024,10025]{1,0:T(8,128)(2,1)} async-done(((bf16[16,10025]{1,0:T(8,128)(2,1)}), bf16[1024,10025]{1,0:T(8,128)(2,1)}) %all-gather.2.cloned.1.call-update) | async-done | bytes 20531216 | tf_op jit(solution)/shard_map/all_gather | solution.py:22
  267.0 11.9 %fusion = f32[128,1024]{1,0:T(8,128)} fusion(bf16[128,10025]{1,0:T(8,128)(2,1)S(1)} %bitcast_multiply_fusion, bf16[1024,10025]{1,0:T(8,128)(2,1)} %all-gather.2.cloned.1.call-done), kind=kOutput, calls=%fused_computation.8 | convolution fusion | flops 2627993600 | bytes 23621888 | tf_op jit(solution)/shard_map/dot_general | solution.py:10
  278.8 0.0 reduce-scatter.2.cloned.1.call-update
  278.9 0.0 copy-done.1
  278.9 0.0 copy-done.2
  278.9 0.2 select_reduce_fusion
  279.1 0.0 copy-done.3
  279.1 0.0 copy-start
  279.1 112.7 %reduce-scatter.2.cloned.1.call-done = f32[16,1024]{1,0:T(8,128)} async-done(((f32[128,1024]{1,0:T(8,128)}), f32[16,1024]{1,0:T(8,128)}) %reduce-scatter.2.cloned.1.call-update) | async-done | bytes 65552 | tf_op jit(solution)/shard_map/reduce_scatter | solution.py:24
  391.8 1.0 reshape.27
  392.8 0.3 copy.14
  393.2 2.4 scatter_fusion
  395.6 0.2 copy.15
  395.8 0.3 reshape.25
  396.1 0.0 copy-done
  396.1 0.7 subtract_divide_fusion
  (3 shorter events, 0.1 us)
Async XLA Ops:
  6.5 260.4 %all-gather.2.cloned.1.call-start = ((), (), s32[]{:S(2)}) async-start(), calls=%async_computation.2 | async-start | bytes 21032960 | tf_op jit(solution)/shard_map/all_gather | solution.py:22
  13.9 84.1 %all-to-all-start = ((bf16[16,8,10025]{2,0,1:T(8,128)(2,1)}), bf16[16,8,10025]{2,0,1:T(8,128)(2,1)}, u32[]{:S(2)}, u32[]{:S(2)}) async-start(bf16[16,8,10025]{2,0,1:T(8,128)(2,1)} %copy.13), calls=%async_computation | async-start | bytes 5177344 | tf_op jit(solution)/shard_map/all_to_all | solution.py:16
  31.6 360.2 %reduce-scatter.2.cloned.1.call-start = ((), (), s32[]{:S(2)}) async-start(), calls=%async_computation.3 | async-start | bytes 589824 | tf_op jit(solution)/shard_map/reduce_scatter | solution.py:24
  100.0 178.8 %copy-start.1 = (s32[16,2]{0,1:T(2,128)S(1)}, s32[16,2]{0,1:T(2,128)}, u32[]{:S(2)}) copy-start(s32[16,2]{0,1:T(2,128)} %param.9) | copy-start | bytes 388
  100.0 178.8 %copy-start.2 = (f32[120]{0:T(128)S(1)}, f32[120]{0:T(128)}, u32[]{:S(2)}) copy-start(f32[120]{0:T(128)} %param.10) | copy-start | bytes 1444
  100.1 179.0 %copy-start.3 = (s32[64]{0:T(128)S(1)}, s32[64]{0:T(128)}, u32[]{:S(2)}) copy-start(s32[64]{0:T(128)} %param.8) | copy-start | bytes 772
  279.1 117.0 %copy-start = (f32[1024]{0:T(1024)S(1)}, f32[1024]{0:T(1024)}, u32[]{:S(2)}) copy-start(f32[1024]{0:T(1024)} %param.11) | copy-start | bytes 12292
Sparse Core Ops, SparseCore 0:
  9.5 257.4 all-gather.1
  279.0 112.7 reduce-scatter.1
where the time goes:
time: 404 us
  waiting for transfers between devices  347 us (86%)
  starting transfers between devices  17.8 us (4%)
  between operations  13.5 us (3%)
  matrix products  11.9 us (3%)
  local copies, waits for them, and re-layouts  10.9 us (3%)
    all_gather x1, waiting for transfers between devices, per_device(): gathered = lax.all_gather(ints, 'blk', axis=0, tiled=True)  167 us
    reduce_scatter x1, waiting for transfers between devices, per_device(): summed = lax.psum_scatter(stored, 'pair', scatter_dimension=0, tiled=True)  113 us
    all_to_all x1, waiting for transfers between devices, per_device(): lax.all_to_all(amps, 'pair', split_axis=1, concat_axis=0, tiled=True)  66.3 us
    all_to_all x1, starting transfers between devices, per_device(): lax.all_to_all(amps, 'pair', split_axis=1, concat_axis=0, tiled=True)  17.7 us
    dot_general x1, matrix products, contract(): lax.dot_general(weighted, slab_part, (((1,), (1,)), ((), ())), preferred_...  11.9 us
  transfers between devices with their start and end apart: 3, of which 3 were waited for; matrix products, arithmetic and copies ran while one was open for 1% of the time, Pallas kernels for 0%

commit v1 on v0

--- a/solution.py
+++ b/solution.py
@@ -4,6 +4,13 @@
 from jax.sharding import PartitionSpec as P
 
 NV = 400
+
+
+def swapped_in(x, axis, d):
+    size = lax.axis_size(axis)
+    pieces = jnp.stack([x for _ in range(size)])
+    pieces = lax.all_to_all(pieces, axis, split_axis=0, concat_axis=0)
+    return jnp.concatenate(pieces, axis=d)
 
 
 def contract(weighted, slab_part):
@@ -19,7 +26,7 @@
         jnp.int32, (1, shard_width), 1
     )
     weighted = relaid * jnp.where(column < NV, 1.0, 2.0).astype(jnp.bfloat16)
-    gathered = lax.all_gather(ints, "blk", axis=0, tiled=True)
+    gathered = swapped_in(ints, "blk", 0)
     stored = contract(weighted, gathered)
     summed = lax.psum_scatter(stored, "pair", scatter_dimension=0, tiled=True)
     blocks = block_of.shape[0]

time: 404 us -> 1200 us (2.97)
  waiting for transfers between devices: 347 us -> 1000 us
  blocking collectives: 0 us -> 80.3 us
  starting transfers between devices: 17.8 us -> 70 us
    all_to_all x1, waiting for transfers between devices: 66.3 us -> 899 us  [swapped_in(): pieces = lax.all_to_all(pieces, axis, split_axis=0, concat_axis=0)]
    all_gather x1 -> x0, waiting for transfers between devices: 167 us -> none  [per_device(): gathered = lax.all_gather(ints, 'blk', axis=0, tiled=True)]
    all_to_all x0 -> x1, blocking collectives: none -> 80.3 us  [per_device(): lax.all_to_all(amps, 'pair', split_axis=1, concat_axis=0, tiled=True)]
    all_to_all x1, starting transfers between devices: 17.7 us -> 69.9 us  [swapped_in(): pieces = lax.all_to_all(pieces, axis, split_axis=0, concat_axis=0)]
  transfers between devices with their start and end apart: 3 -> 2, of which waited for: 3 -> 2; matrix products, arithmetic and copies ran while one was open for 1% -> 0% of each run, Pallas kernels for 0% -> 0%
where the time goes in v1:
time: 1200 us
  waiting for transfers between devices  1000 us (83%)
  blocking collectives  80.3 us (7%)
  starting transfers between devices  70 us (6%)
  local copies, waits for them, and re-layouts  16.5 us (1%)
  between operations  13.5 us (1%)
    all_to_all x1, waiting for transfers between devices, swapped_in(): pieces = lax.all_to_all(pieces, axis, split_axis=0, concat_axis=0)  899 us
    reduce_scatter x1, waiting for transfers between devices, per_device(): summed = lax.psum_scatter(stored, 'pair', scatter_dimension=0, tiled=True)  101 us
    all_to_all x1, blocking collectives, per_device(): lax.all_to_all(amps, 'pair', split_axis=1, concat_axis=0, tiled=True)  80.3 us
    all_to_all x1, starting transfers between devices, swapped_in(): pieces = lax.all_to_all(pieces, axis, split_axis=0, concat_axis=0)  69.9 us
  transfers between devices with their start and end apart: 2, of which 2 were waited for; matrix products, arithmetic and copies ran while one was open for 0% of the time, Pallas kernels for 0%

profile of v1, /device:TPU:2, one launch (start us, length us, event | category | flops | bytes accessed | tf_op | source)
XLA Modules:
  0.0 1195.7 jit_solution(2238124568183181606)
XLA Ops:
  6.5 4.8 all_to_all.13
  11.4 0.3 copy.13
  11.6 0.0 copy-start
  11.6 80.3 %all_to_all.18 = bf16[16,8,10025]{2,0,1:T(8,128)(2,1)} all-to-all(bf16[16,8,10025]{2,0,1:T(8,128)(2,1)S(1)} %copy.13), channel_id=1, replica_groups=mesh['pair'=8,'blk'=64] {'pair'}, dimensions={1} | all-to-all | bytes 5132800 | tf_op jit(solution)/shard_map/all_to_all | solution.py:23
  92.0 0.0 copy-done
  92.0 7.2 stack.2
  99.2 69.9 %all-to-all-start.1 = ((bf16[64,16,10025]{2,1,0:T(8,128)(2,1)}), bf16[64,16,10025]{2,1,0:T(8,128)(2,1)}, u32[]{:S(2)}, u32[]{:S(2)}) async-start(bf16[64,16,10025]{2,1,0:T(8,128)(2,1)} %stack.2), calls=%async_computation.1 | async-start | bytes 41418752 | tf_op jit(solution)/shard_map/all_to_all | solution.py:12
  169.1 0.0 reduce-scatter.2.cloned.1.call-start
  169.2 2.1 broadcast_multiply_fusion
  171.2 899.1 %all-to-all-done.1 = bf16[64,16,10025]{2,1,0:T(8,128)(2,1)} async-done(((bf16[64,16,10025]{2,1,0:T(8,128)(2,1)}), bf16[64,16,10025]{2,1,0:T(8,128)(2,1)}, u32[]{:S(2)}, u32[]{:S(2)}) %all-to-all-start.1) | async-done | bytes 20531232 | tf_op jit(solution)/shard_map/all_to_all | solution.py:12
  1070.4 0.0 copy-start.2
  1070.4 0.0 copy-start.3
  1070.4 0.0 copy-start.4
  1070.4 11.9 fusion
  1082.3 0.0 reduce-scatter.2.cloned.1.call-update
  1082.3 0.0 copy-done.2
  1082.3 0.0 copy-done.3
  1082.3 0.2 select_reduce_fusion
  1082.5 0.0 copy-done.4
  1082.5 0.0 copy-start.1
  1082.5 101.3 %reduce-scatter.2.cloned.1.call-done = f32[16,1024]{1,0:T(8,128)} async-done(((f32[128,1024]{1,0:T(8,128)}), f32[16,1024]{1,0:T(8,128)}) %reduce-scatter.2.cloned.1.call-update) | async-done | bytes 65552 | tf_op jit(solution)/shard_map/reduce_scatter | solution.py:31
  1183.8 1.0 reshape.39
  1184.9 0.3 copy.14
  1185.2 2.4 scatter_fusion
  1187.7 0.2 copy.15
  1187.8 0.3 reshape.37
  1188.1 0.0 copy-done.1
  1188.1 0.7 subtract_divide_fusion
  (3 shorter events, 0.1 us)
Async XLA Ops:
  11.6 80.3 %copy-start = (bf16[16,10025]{1,0:T(8,128)(2,1)S(1)}, bf16[16,10025]{1,0:T(8,128)(2,1)}, u32[]{:S(2)}) copy-start(bf16[16,10025]{1,0:T(8,128)(2,1)} %param.7) | copy-start | bytes 962404
  99.2 971.2 %all-to-all-start.1 = ((bf16[64,16,10025]{2,1,0:T(8,128)(2,1)}), bf16[64,16,10025]{2,1,0:T(8,128)(2,1)}, u32[]{:S(2)}, u32[]{:S(2)}) async-start(bf16[64,16,10025]{2,1,0:T(8,128)(2,1)} %stack.2), calls=%async_computation.1 | async-start | bytes 41418752 | tf_op jit(solution)/shard_map/all_to_all | solution.py:12
  169.1 1014.7 %reduce-scatter.2.cloned.1.call-start = ((), (), s32[]{:S(2)}) async-start(), calls=%async_computation.3 | async-start | bytes 589824 | tf_op jit(solution)/shard_map/reduce_scatter | solution.py:31
  1070.4 12.0 copy-start.2
  1070.4 12.0 %copy-start.3 = (f32[120]{0:T(128)S(1)}, f32[120]{0:T(128)}, u32[]{:S(2)}) copy-start(f32[120]{0:T(128)} %param.10) | copy-start | bytes 1444
  1070.4 12.2 %copy-start.4 = (s32[64]{0:T(128)S(1)}, s32[64]{0:T(128)}, u32[]{:S(2)}) copy-start(s32[64]{0:T(128)} %param.8) | copy-start | bytes 772
  1082.5 105.6 %copy-start.1 = (f32[1024]{0:T(1024)S(1)}, f32[1024]{0:T(1024)}, u32[]{:S(2)}) copy-start(f32[1024]{0:T(1024)} %param.11) | copy-start | bytes 12292
Sparse Core Ops, SparseCore 0:
  1082.4 101.3 reduce-scatter.1
